TPU v7x, 32 devices: a whole 2x2x4 slice. The times are simulated.
32 devices in a mesh: gx: 8 (over z, x), gy: 4 (over y, core).
Axes of the slice: x: 2, y: 2, z: 4, core: 2. Of those that a mesh axis runs over, the one named last changes fastest.
Arguments:
- a_blocks: bfloat16 [8, 32, 64, 448], P('gx', 'gy'), may hold values from -0.25 to 0.25
- a_cols: int32 [8, 32, 7], P('gx', 'gy'), may hold values from 0 to 15
- mushy: int32 [8, 32], P('gx', 'gy'), may hold values 0 or 1
- p_blocks: bfloat16 [8, 32, 64, 256], P('gx', 'gy'), may hold values from -0.375 to 0.375
- p_cols: int32 [8, 32, 4], P('gx', 'gy'), may hold values from 0 to 7
- send_rows: int32 [8, 32], P('gx', 'gy'), may hold values from 0 to 7
Outputs:
- coarse_tiles: float32 [8, 512, 1536], P('gx', 'gy')
All inputs are finite; a program needn't handle non-finite values. No bound on the sum of `mushy` on one device may be relied on, other than what follows from the above.
Results may differ from a plain program's by a relative error of at most 0.0038.
Values may be sent and summed in bfloat16 or wider, within the bound.
No kernel may reach another device: no remote copies, remote signals or barrier semaphores. Data moves between devices by JAX's collectives and lax.ppermute only.
A program may use at most 64 MiB of HBM per device.

v0:
```python
import functools

import jax
import jax.numpy as jnp
from jax import lax
from jax.experimental import pallas as pl
from jax.experimental.pallas import tpu as pltpu
from jax.sharding import PartitionSpec as P

KA = 7
KS = 3
NCOL = 8
LANES = 128
WIDE = 256

F32 = jnp.float32
BF16 = jnp.bfloat16
SMEM = pl.BlockSpec(memory_space=pltpu.SMEM)
VMEM = pl.BlockSpec(memory_space=pltpu.VMEM)
HBM = pl.BlockSpec(memory_space=pltpu.HBM)
LONG = pl.CostEstimate(flops=10000000000, bytes_accessed=1000000, transcendentals=0)
SHORT = pl.CostEstimate(flops=1000000000, bytes_accessed=1000000, transcendentals=0)
PARAMS = pltpu.CompilerParams(vmem_limit_bytes=24 * 1024 * 1024)


def spread(value, masks_of, width):
    size = value.shape[0]
    row = lax.broadcasted_iota(jnp.int32, (size, WIDE), 0)
    lane = lax.broadcasted_iota(jnp.int32, (size, WIDE), 1)
    unit = jnp.where(row == lane % size, 1.0, 0.0).astype(BF16)
    tiles = []
    for c in range(width // WIDE):
        moves = jnp.concatenate([unit * mask for mask in masks_of(c * WIDE // size)], axis=0)
        tiles.append(jnp.dot(value, moves, preferred_element_type=F32))
    return tiles


def masks_at(cols, size, dtype):
    slots = (lax.broadcasted_iota(jnp.int32, (1, WIDE), 1) // size).astype(dtype)
    return lambda first: [
        jnp.where(slots == col - first, 1.0, 0.0).astype(BF16) for col in cols
    ]


def multiply(acol, mush, a_ref, base, ext_ref, prod_ref):
    rows, size = a_ref.shape[0], a_ref.shape[1]
    ext_ref[ext_ref.shape[0] - 1] = jnp.zeros(ext_ref.shape[1:], BF16)
    none = ext_ref.shape[0] - 1
    for n in range(rows):
        limit = jnp.where(mush[n] > 0, KA, KS)
        picks = []
        for k in range(KA):
            spot = acol[k, 0, n] - base
            good = (k < limit) & (spot >= 0) & (spot < none)
            picks.append(jnp.where(good, spot, none))
        picked = jnp.concatenate([ext_ref[spot] for spot in picks], axis=0)
        value = jnp.dot(a_ref[n], picked, preferred_element_type=F32)
        prod_ref[n * size : (n + 1) * size, :] = value.astype(BF16)


def finish(ownt_ref, prod, keep_ref, send_ref):
    rows = ownt_ref.shape[0] // 2
    sent = jnp.dot(ownt_ref[rows:, :], prod, preferred_element_type=F32)
    send_ref[...] = sent.astype(BF16).reshape(send_ref.shape)
    kept = jnp.dot(ownt_ref[:rows, :], prod, preferred_element_type=F32)
    keep_ref[...] = kept.reshape(keep_ref.shape)


def pack_kernel(sends_in, pcol_in, p_in, first_ref, second_ref, sends, pcol, p_ref, packed_ref, sems):
    copies = [
        pltpu.make_async_copy(src, dst, sems.at[i])
        for i, (src, dst) in enumerate(((sends_in, sends), (pcol_in, pcol), (p_in, p_ref)))
    ]
    for copy in copies:
        copy.start()
    for copy in copies[:2]:
        copy.wait()
    odd = lax.axis_index("gx") % 2
    count = sends.shape[0] // 2
    size = p_ref.shape[1]
    slots = pcol.shape[0]
    starts = ((1 - odd) * count, odd * count)
    tail = packed_ref.shape[1] - count * size
    which = lax.broadcasted_iota(jnp.int32, (tail, packed_ref.shape[2]), 0)
    for i, start in enumerate(starts):
        cols = jnp.zeros(which.shape, F32)
        for s in range(count):
            row = sends[start + s]
            for j in range(slots):
                cols = jnp.where(which == s * slots + j, pcol[j, row].astype(F32), cols)
        packed_ref[i, count * size :, :] = cols.astype(BF16)
    copies[2].wait()
    copies = []
    for i, (out_ref, start) in enumerate(zip((first_ref, second_ref), starts)):
        for s in range(count):
            packed_ref[i, s * size : (s + 1) * size, :] = p_ref[sends[start + s]]
        copies.append(pltpu.make_async_copy(packed_ref.at[i], out_ref, sems.at[i]))
        copies[-1].start()
    for copy in copies:
        copy.wait()


def own_kernel(parts, acol, mush, pcol, a_ref, p_ref, passed, ownt_ref, keep_ref, send_ref, *refs):
    own_ref, prod_ref = refs[-2:]
    bit = lax.axis_index("gy") % 2
    rows, size = p_ref.shape[0], p_ref.shape[1]
    width = NCOL * size
    share = width // parts
    for n in range(rows):
        masks = masks_at([pcol[j, n] for j in range(pcol.shape[0])], size, jnp.int32)
        for c, tile in enumerate(spread(p_ref[n], masks, width)):
            own_ref[n, :, c * WIDE : (c + 1) * WIDE] = tile.astype(BF16)
    for c in range(width // LANES):
        column = own_ref[:rows, :, c * LANES : (c + 1) * LANES]
        flipped = column.reshape(rows * size, LANES).T
        for k in range(LANES // share):
            part = c * (LANES // share) + k
            spot = part // 2 + jnp.where(part % 2 == bit, 0, parts // 2)
            at = pl.ds(pl.multiple_of(spot * share, share), share)
            ownt_ref[at, :] = flipped[k * share : (k + 1) * share, :]
    multiply(acol, mush, a_ref, 0, own_ref, prod_ref)
    finish(ownt_ref, prod_ref[...], keep_ref, send_ref)


def scatter_kernel(acol, mush, a_ref, high_ref, low_ref):
    odd = lax.axis_index("gx") % 2
    rows, size = a_ref.shape[0], a_ref.shape[1]
    width = high_ref.shape[2]
    for n in range(rows):
        limit = jnp.where(mush[n] > 0, KA, KS)
        at = slice(n * size, (n + 1) * size)
        for order in range(2):
            right = odd if order else 1 - odd
            base = rows + right * (width // size)
            cols = [jnp.where(k < limit, acol[k, 0, n] - base, -1) for k in range(KA)]
            masks = masks_at(cols, size, jnp.int32)
            for c, tile in enumerate(spread(a_ref[n], masks, width)):
                spot = slice(c * WIDE, (c + 1) * WIDE)
                high = tile.astype(BF16)
                high_ref[order, at, spot] = high
                low_ref[order, at, spot] = (tile - high.astype(F32)).astype(BF16)


def ghost_kernel(order, high_ref, low_ref, in_ref, ownt_ref, *refs):
    keep_ref, send_ref, ext_ref, prod_ref = refs[-4:]
    width = ownt_ref.shape[0]
    size = width // NCOL
    slots = in_ref.shape[1] // size
    count = ext_ref.shape[0] // size
    cols = in_ref[count * size :, :].astype(F32)
    for n in range(count):
        at = slice(n * size, (n + 1) * size)
        masks = masks_at([cols[n * slots + j : n * slots + j + 1, :] for j in range(slots)], size, F32)
        for c, tile in enumerate(spread(in_ref[at, :], masks, width)):
            ext_ref[at, c * WIDE : (c + 1) * WIDE] = tile.astype(BF16)
    ext = ext_ref[...]
    step = prod_ref.shape[0] // 2
    for m in range(2):
        at = slice(m * step, (m + 1) * step)
        value = jnp.dot(high_ref[order, at, :], ext, preferred_element_type=F32)
        value += jnp.dot(low_ref[order, at, :], ext, preferred_element_type=F32)
        prod_ref[at, :] = value.astype(BF16)
    finish(ownt_ref, prod_ref[...], keep_ref, send_ref)


def fold_kernel(stage, keep_ref, recv_ref, *refs):
    next_ref, send_ref = refs[-2:]
    bit = (lax.axis_index("gy") >> stage) % 2
    for i in range(next_ref.shape[0]):
        mine, other = 2 * i + bit, 2 * i + 1 - bit
        send_ref[i] = (keep_ref[other] + recv_ref[other].astype(F32)).astype(BF16)
        next_ref[i] = keep_ref[mine] + recv_ref[mine].astype(F32)


def write_kernel(order, keep_ref, recv_ref, *refs):
    sum_ref, sem = refs[-2:]
    out_ref = refs[0 if order is None else 1]
    odd = lax.axis_index("gx") % 2
    third = 1 if order is None else 2 * odd if order else 2 - 2 * odd
    width = sum_ref.shape[1]
    sum_ref[...] = keep_ref[0] + recv_ref[0].astype(F32)
    spot = pl.ds(pl.multiple_of(third * width, width), width)
    copy = pltpu.make_async_copy(sum_ref, out_ref.at[:, spot], sem)
    copy.start()
    if order is None:
        refs[1][...] = jnp.zeros(refs[1].shape, F32)
    copy.wait()


def swapped(value, axis, step):
    length = lax.axis_size(axis)
    return lax.ppermute(value, axis, [(i, i ^ step) for i in range(length) if i ^ step < length])


def folded(keep, send, parts, after=()):
    left, share, width = keep.shape
    stage = 0
    while left > 1:
        recv = swapped(send, "gy", 1 << stage)
        stage += 1
        left //= 2
        keep, send = pl.pallas_call(
            functools.partial(fold_kernel, stage),
            out_shape=(
                jax.ShapeDtypeStruct((left, share, width), F32),
                jax.ShapeDtypeStruct((left, share, width), BF16),
            ),
            in_specs=[VMEM] * (2 + len(after)),
            out_specs=(VMEM, VMEM),
            compiler_params=PARAMS,
            name="fold",
        )(keep, recv, *after)
        after = ()
    return keep, swapped(send, "gy", 1 << stage), keep


def written(order, keep, recv, result):
    share, width = keep.shape[1:]
    start = order is None
    whole = jax.ShapeDtypeStruct((share, 3 * width), F32)
    token = jax.ShapeDtypeStruct((8, LANES), F32)
    return pl.pallas_call(
        functools.partial(write_kernel, order),
        out_shape=(whole, token) if start else whole,
        in_specs=[VMEM, VMEM] if start else [VMEM, VMEM, HBM],
        out_specs=(HBM, VMEM) if start else HBM,
        input_output_aliases={} if start else {2: 0},
        scratch_shapes=[pltpu.VMEM((share, width), F32), pltpu.SemaphoreType.DMA],
        compiler_params=PARAMS,
        cost_estimate=LONG,
        name="write",
    )(keep, recv, *([] if start else [result]))


def body(a_blocks, a_cols, mushy, p_blocks, p_cols, send_rows):
    rows, size, inner = p_blocks.shape[1:]
    acol, pcol = a_cols.transpose(2, 0, 1), p_cols[0].T
    mush, sends = mushy[0], send_rows[0]
    ablk, pblk = a_blocks[0], p_blocks[0]
    count = sends.shape[0] // 2
    width = NCOL * size
    length = lax.axis_size("gx")
    parts = lax.axis_size("gy")
    share = width // parts

    tail = -(-count * pcol.shape[0] // 16) * 16
    packed = jax.ShapeDtypeStruct((count * size + tail, inner), BF16)

    first, second = pl.pallas_call(
        pack_kernel,
        out_shape=(packed, packed),
        in_specs=[HBM] * 3,
        out_specs=(HBM, HBM),
        scratch_shapes=[
            pltpu.SMEM(sends.shape, sends.dtype),
            pltpu.SMEM(pcol.shape, pcol.dtype),
            pltpu.VMEM(pblk.shape, BF16),
            pltpu.VMEM((2,) + packed.shape, BF16),
            pltpu.SemaphoreType.DMA((3,)),
        ],
        compiler_params=pltpu.CompilerParams(vmem_limit_bytes=56 * 1024 * 1024),
        cost_estimate=LONG,
        name="pack",
    )(sends, pcol, pblk)
    even = [(i, i + 1) for i in range(0, length - 1, 2)]
    uneven = [(i, i + 1) for i in range(1, length - 1, 2)]
    first = lax.ppermute(first, "gx", even + [(j, i) for i, j in even])

    partial = (
        jax.ShapeDtypeStruct((parts // 2, share, width), F32),
        jax.ShapeDtypeStruct((parts // 2, share, width), BF16),
    )
    own_t, keep, send, second = pl.pallas_call(
        functools.partial(own_kernel, parts),
        out_shape=(jax.ShapeDtypeStruct((width, rows * size), BF16),) + partial + (packed,),
        in_specs=[SMEM, SMEM, SMEM, VMEM, VMEM, HBM],
        out_specs=(VMEM, VMEM, VMEM, HBM),
        input_output_aliases={5: 3},
        scratch_shapes=[
            pltpu.VMEM((rows + 1, size, width), BF16),
            pltpu.VMEM((rows * size, width), BF16),
        ],
        compiler_params=PARAMS,
        cost_estimate=SHORT,
        name="own",
    )(acol, mush, pcol, ablk, pblk, second)
    second = lax.ppermute(second, "gx", uneven + [(j, i) for i, j in uneven])
    keep, recv, folds = folded(keep, send, parts)
    split = jax.ShapeDtypeStruct((2, rows * size, count * size), BF16)
    high, low = pl.pallas_call(
        scatter_kernel,
        out_shape=(split, split),
        in_specs=[SMEM, SMEM, VMEM],
        out_specs=(VMEM, VMEM),
        compiler_params=PARAMS,
        cost_estimate=LONG,
        name="scatter",
    )(acol, mush, ablk)
    pieces = []
    for order, ghosts in enumerate((first, second)):
        after = [] if order else [folds]
        pieces.append(
            pl.pallas_call(
                functools.partial(ghost_kernel, order),
                out_shape=partial,
                in_specs=[VMEM] * (4 + len(after)),
                out_specs=(VMEM, VMEM),
                scratch_shapes=[
                    pltpu.VMEM((count * size, width), BF16),
                    pltpu.VMEM((rows * size, width), BF16),
                ],
                compiler_params=PARAMS,
                cost_estimate=LONG,
                name="ghost",
            )(high, low, ghosts, own_t, *after)
        )
    result, token = written(None, keep, recv, None)
    sides = [folded(*pieces[0], parts), folded(*pieces[1], parts, (token,))]
    for order, (keep, recv, folds) in enumerate(sides):
        result = written(order, keep, recv, result)
    return result[None]


def solution(mesh):
    placed = (
        P("gx", "gy", None, None),
        P("gx", "gy", None),
        P("gx", "gy"),
        P("gx", "gy", None, None),
        P("gx", "gy", None),
        P("gx", "gy"),
    )
    return jax.shard_map(
        body, mesh=mesh, in_specs=placed, out_specs=P("gx", "gy", None), check_vma=False
    )
```

profile of v0, /device:TPU:24, one launch (start us, length us, event | category | flops | bytes accessed | tf_op | source)
XLA Modules:
  0.0 25.1 jit_solution(16720258496808218647)
XLA Ops:
  0.0 1.8 %pack.1 = (bf16[272,256]{1,0:T(8,128)(2,1)}, bf16[272,256]{1,0:T(8,128)(2,1)}) custom-call(s32[8]{0:T(128)} %bitcast.19, s32[4,8]{1,0:T(4,128)} %bitcast.15, bf16[8,64,256]{2,1,0:T(8,128)(2,1)} %bitcast.11), custom_call_target="tpu_custom_call" | custom-call | flops 10000000000 | bytes 1000000 | tf_op jit(solution)/shard_map/pack/pallas_call | solution.py:249
  1.8 1.6 %collective-permute-start.5 = (bf16[272,256]{1,0:T(8,128)(2,1)}, bf16[272,256]{1,0:T(8,128)(2,1)S(1)}, u32[]{:S(2)}, u32[]{:S(2)}) collective-permute-start(bf16[272,256]{1,0:T(8,128)(2,1)} %get-tuple-element.39), channel_id=1, source_target_pairs={{0,4},{8,12},{16,20},{24,28},{4,0},{12,8},{20,16},{28,24},{1,5},{9... | collective-permute-start | bytes 417800 | tf_op jit(solution)/shard_map/ppermute | solution.py:267
  3.4 0.7 %copy-done.3 = s32[1,8,4]{1,2,0:T(4,128)S(1)} copy-done((s32[1,8,4]{1,2,0:T(4,128)S(1)}, s32[1,8,4]{1,2,0:T(4,128)}, u32[]{:S(2)}) %copy-start.3) | copy-done | bytes 152
  4.0 2.3 %own.1 = (bf16[512,512]{1,0:T(8,128)(2,1)S(1)}, f32[2,128,512]{2,1,0:T(8,128)S(1)}, bf16[2,128,512]{2,1,0:T(8,128)(2,1)S(1)}, bf16[272,256]{1,0:T(8,128)(2,1)}) custom-call(s32[7,1,8]{2,1,0:T(1,128)S(1)} %bitcast.13, s32[8]{0:T(128)S(1)} %bitcast.17, s32[4,8]{1,0:T(4,128)S(1)} %bitcast.16, ...), custom_call_target="tpu_custom_call", output_to_operand_aliasing={{3}: (5, {})} | custom-call | flops 1000000000 | bytes 1000000 | tf_op jit(solution)/shard_map/own/pallas_call | solution.py:273
  6.3 2.3 %collective-permute-start = (bf16[272,256]{1,0:T(8,128)(2,1)}, bf16[272,256]{1,0:T(8,128)(2,1)S(1)}, u32[]{:S(2)}, u32[]{:S(2)}) collective-permute-start(bf16[272,256]{1,0:T(8,128)(2,1)} %get-tuple-element.28), channel_id=1, source_target_pairs={{4,8},{12,16},{20,24},{8,4},{16,12},{24,20},{5,9},{13,17},{21,25},... | collective-permute-start | bytes 417800 | tf_op jit(solution)/shard_map/ppermute | solution.py:287
  8.6 0.1 collective-permute-start.2
  8.7 1.4 %scatter.1 = (bf16[2,512,256]{2,1,0:T(8,128)(2,1)S(1)}, bf16[2,512,256]{2,1,0:T(8,128)(2,1)S(1)}) custom-call(s32[7,1,8]{2,1,0:T(1,128)S(1)} %bitcast.14, s32[8]{0:T(128)S(1)} %bitcast.18, bf16[8,64,448]{2,1,0:T(8,128)(2,1)S(1)} %bitcast.10), custom_call_target="tpu_custom_call" | custom-call | flops 10000000000 | bytes 1000000 | tf_op jit(solution)/shard_map/scatter/pallas_call | solution.py:290
  10.1 0.1 collective-permute-done.2.recv_ref
  10.2 0.1 fold.3
  10.3 1.6 %collective-permute-start.3 = (bf16[1,128,512]{2,1,0:T(8,128)(2,1)S(1)}, bf16[1,128,512]{2,1,0:T(8,128)(2,1)S(1)}, u32[]{:S(2)}, u32[]{:S(2)}) collective-permute-start(bf16[1,128,512]{2,1,0:T(8,128)(2,1)S(1)} %get-tuple-element.35), channel_id=1, source_target_pairs={{0,2},{1,3},{2,0},{3,1},{4,6},{5,7},{6,4},{7,5},{8,10},{9,11},{10,... | collective-permute-start | bytes 393224 | tf_op jit(solution)/shard_map/ppermute | solution.py:192
  11.9 1.0 %ghost.3 = (f32[2,128,512]{2,1,0:T(8,128)S(1)}, bf16[2,128,512]{2,1,0:T(8,128)(2,1)S(1)}) custom-call(bf16[2,512,256]{2,1,0:T(8,128)(2,1)S(1)} %get-tuple-element.25.high_ref, bf16[2,512,256]{2,1,0:T(8,128)(2,1)S(1)} %get-tuple-element.26.low_ref, bf16[272,256]{1,0:T(8,128)(2,1)S(1)} %collective-permute-done.5.in_ref, ...), custom_call_target="tpu_custom_call" | custom-call | flops 10000000000 | bytes 1000000 | tf_op jit(solution)/shard_map/ghost/pallas_call | solution.py:303
  13.0 0.1 collective-permute-start.6
  13.1 1.3 %collective-permute-done.in_ref = bf16[272,256]{1,0:T(8,128)(2,1)S(1)} collective-permute-done((bf16[272,256]{1,0:T(8,128)(2,1)}, bf16[272,256]{1,0:T(8,128)(2,1)S(1)}, u32[]{:S(2)}, u32[]{:S(2)}) %collective-permute-start) | collective-permute-done | bytes 139296 | tf_op jit(solution)/shard_map/ppermute | solution.py:287
  14.4 1.0 %ghost.2 = (f32[2,128,512]{2,1,0:T(8,128)S(1)}, bf16[2,128,512]{2,1,0:T(8,128)(2,1)S(1)}) custom-call(bf16[2,512,256]{2,1,0:T(8,128)(2,1)S(1)} %get-tuple-element.25.high_ref, bf16[2,512,256]{2,1,0:T(8,128)(2,1)S(1)} %get-tuple-element.26.low_ref, bf16[272,256]{1,0:T(8,128)(2,1)S(1)} %collective-permute-done.in_ref, ...), custom_call_target="tpu_custom_call" | custom-call | flops 10000000000 | bytes 1000000 | tf_op jit(solution)/shard_map/ghost/pallas_call | solution.py:303
  15.5 0.1 collective-permute-start.1
  15.6 0.1 fold.5
  15.7 1.6 %collective-permute-start.7 = (bf16[1,128,512]{2,1,0:T(8,128)(2,1)S(1)}, bf16[1,128,512]{2,1,0:T(8,128)(2,1)S(1)}, u32[]{:S(2)}, u32[]{:S(2)}) collective-permute-start(bf16[1,128,512]{2,1,0:T(8,128)(2,1)S(1)} %get-tuple-element.43), channel_id=1, source_target_pairs={{0,2},{1,3},{2,0},{3,1},{4,6},{5,7},{6,4},{7,5},{8,10},{9,11},{10,... | collective-permute-start | bytes 393224 | tf_op jit(solution)/shard_map/ppermute | solution.py:192
  17.2 0.7 %write.3 = (f32[128,1536]{1,0:T(8,128)}, f32[8,128]{1,0:T(8,128)S(1)}) custom-call(f32[1,128,512]{2,1,0:T(8,128)S(1)} %get-tuple-element.34.keep_ref.refs_0_, bf16[1,128,512]{2,1,0:T(8,128)(2,1)S(1)} %collective-permute-done.3.recv_ref), custom_call_target="tpu_custom_call" | custom-call | flops 10000000000 | bytes 1000000 | tf_op jit(solution)/shard_map/write/pallas_call | solution.py:222
  18.0 0.1 fold.4
  18.1 0.7 %collective-permute-start.4 = (bf16[1,128,512]{2,1,0:T(8,128)(2,1)S(1)}, bf16[1,128,512]{2,1,0:T(8,128)(2,1)S(1)}, u32[]{:S(2)}, u32[]{:S(2)}) collective-permute-start(bf16[1,128,512]{2,1,0:T(8,128)(2,1)S(1)} %get-tuple-element.38), channel_id=1, source_target_pairs={{0,2},{1,3},{2,0},{3,1},{4,6},{5,7},{6,4},{7,5},{8,10},{9,11},{10,... | collective-permute-start | bytes 393224 | tf_op jit(solution)/shard_map/ppermute | solution.py:192
  18.7 3.3 %collective-permute-done.7.recv_ref = bf16[1,128,512]{2,1,0:T(8,128)(2,1)S(1)} collective-permute-done((bf16[1,128,512]{2,1,0:T(8,128)(2,1)S(1)}, bf16[1,128,512]{2,1,0:T(8,128)(2,1)S(1)}, u32[]{:S(2)}, u32[]{:S(2)}) %collective-permute-start.7) | collective-permute-done | bytes 131104 | tf_op jit(solution)/shard_map/ppermute | solution.py:192
  22.0 0.7 %write.4.refs_0_ = f32[128,1536]{1,0:T(8,128)} custom-call(f32[1,128,512]{2,1,0:T(8,128)S(1)} %get-tuple-element.42.keep_ref, bf16[1,128,512]{2,1,0:T(8,128)(2,1)S(1)} %collective-permute-done.7.recv_ref, f32[128,1536]{1,0:T(8,128)} %get-tuple-element.44.refs_0_), custom_call_target="tpu_custom_call", output_to_operand_aliasing={{}: (2, {})} | custom-call | flops 10000000000 | bytes 1000000 | tf_op jit(solution)/shard_map/write/pallas_call | solution.py:222
  22.8 1.6 %collective-permute-done.4.recv_ref = bf16[1,128,512]{2,1,0:T(8,128)(2,1)S(1)} collective-permute-done((bf16[1,128,512]{2,1,0:T(8,128)(2,1)S(1)}, bf16[1,128,512]{2,1,0:T(8,128)(2,1)S(1)}, u32[]{:S(2)}, u32[]{:S(2)}) %collective-permute-start.4) | collective-permute-done | bytes 131104 | tf_op jit(solution)/shard_map/ppermute | solution.py:192
  24.4 0.7 %write.5 = f32[128,1536]{1,0:T(8,128)} custom-call(f32[1,128,512]{2,1,0:T(8,128)S(1)} %get-tuple-element.37.keep_ref, bf16[1,128,512]{2,1,0:T(8,128)(2,1)S(1)} %collective-permute-done.4.recv_ref, f32[128,1536]{1,0:T(8,128)} %write.4.refs_0_), custom_call_target="tpu_custom_call", output_to_operand_aliasing={{}: (2, {})} | custom-call | flops 10000000000 | bytes 1000000 | tf_op jit(solution)/shard_map/write/pallas_call | solution.py:222
  (13 shorter events, 0.0 us)
Async XLA Ops:
  0.0 3.3 %copy-start = (bf16[1,8,64,448]{3,2,1,0:T(8,128)(2,1)S(1)}, bf16[1,8,64,448]{3,2,1,0:T(8,128)(2,1)}, u32[]{:S(2)}) copy-start(bf16[1,8,64,448]{3,2,1,0:T(8,128)(2,1)} %param.6) | copy-start | bytes 1376260
  0.0 3.3 %copy-start.1 = (bf16[1,8,64,256]{3,2,1,0:T(8,128)(2,1)S(1)}, bf16[1,8,64,256]{3,2,1,0:T(8,128)(2,1)}, u32[]{:S(2)}) copy-start(bf16[1,8,64,256]{3,2,1,0:T(8,128)(2,1)} %param.9) | copy-start | bytes 786436
  1.8 1.6 %copy-start.2 = (s32[1,8,7]{1,0,2:T(1,128)S(1)}, s32[1,8,7]{1,0,2:T(1,128)}, u32[]{:S(2)}) copy-start(s32[1,8,7]{1,0,2:T(1,128)} %param.7) | copy-start | bytes 676
  1.8 10.1 %collective-permute-start.5 = (bf16[272,256]{1,0:T(8,128)(2,1)}, bf16[272,256]{1,0:T(8,128)(2,1)S(1)}, u32[]{:S(2)}, u32[]{:S(2)}) collective-permute-start(bf16[272,256]{1,0:T(8,128)(2,1)} %get-tuple-element.39), channel_id=1, source_target_pairs={{0,4},{8,12},{16,20},{24,28},{4,0},{12,8},{20,16},{28,24},{1,5},{9... | collective-permute-start | bytes 417800 | tf_op jit(solution)/shard_map/ppermute | solution.py:267
  3.3 0.7 %copy-start.3 = (s32[1,8,4]{1,2,0:T(4,128)S(1)}, s32[1,8,4]{1,2,0:T(4,128)}, u32[]{:S(2)}) copy-start(s32[1,8,4]{1,2,0:T(4,128)} %param.10) | copy-start | bytes 388
  3.3 0.7 %copy-start.4 = (s32[1,8]{1,0:T(1,128)S(1)}, s32[1,8]{1,0:T(1,128)}, u32[]{:S(2)}) copy-start(s32[1,8]{1,0:T(1,128)} %param.8) | copy-start | bytes 100
  6.3 8.1 %collective-permute-start = (bf16[272,256]{1,0:T(8,128)(2,1)}, bf16[272,256]{1,0:T(8,128)(2,1)S(1)}, u32[]{:S(2)}, u32[]{:S(2)}) collective-permute-start(bf16[272,256]{1,0:T(8,128)(2,1)} %get-tuple-element.28), channel_id=1, source_target_pairs={{4,8},{12,16},{20,24},{8,4},{16,12},{24,20},{5,9},{13,17},{21,25},... | collective-permute-start | bytes 417800 | tf_op jit(solution)/shard_map/ppermute | solution.py:287
  8.6 1.6 %collective-permute-start.2 = (bf16[2,128,512]{2,1,0:T(8,128)(2,1)S(1)}, bf16[2,128,512]{2,1,0:T(8,128)(2,1)S(1)}, u32[]{:S(2)}, u32[]{:S(2)}) collective-permute-start(bf16[2,128,512]{2,1,0:T(8,128)(2,1)S(1)} %get-tuple-element.33), channel_id=1, source_target_pairs={{0,1},{1,0},{2,3},{3,2},{4,5},{5,4},{6,7},{7,6},{8,9},{9,8},{10,11... | collective-permute-start | bytes 786440 | tf_op jit(solution)/shard_map/ppermute | solution.py:192
  10.3 6.9 %collective-permute-start.3 = (bf16[1,128,512]{2,1,0:T(8,128)(2,1)S(1)}, bf16[1,128,512]{2,1,0:T(8,128)(2,1)S(1)}, u32[]{:S(2)}, u32[]{:S(2)}) collective-permute-start(bf16[1,128,512]{2,1,0:T(8,128)(2,1)S(1)} %get-tuple-element.35), channel_id=1, source_target_pairs={{0,2},{1,3},{2,0},{3,1},{4,6},{5,7},{6,4},{7,5},{8,10},{9,11},{10,... | collective-permute-start | bytes 393224 | tf_op jit(solution)/shard_map/ppermute | solution.py:192
  13.0 2.6 %collective-permute-start.6 = (bf16[2,128,512]{2,1,0:T(8,128)(2,1)S(1)}, bf16[2,128,512]{2,1,0:T(8,128)(2,1)S(1)}, u32[]{:S(2)}, u32[]{:S(2)}) collective-permute-start(bf16[2,128,512]{2,1,0:T(8,128)(2,1)S(1)} %get-tuple-element.41), channel_id=1, source_target_pairs={{0,1},{1,0},{2,3},{3,2},{4,5},{5,4},{6,7},{7,6},{8,9},{9,8},{10,11... | collective-permute-start | bytes 786440 | tf_op jit(solution)/shard_map/ppermute | solution.py:192
  15.5 2.5 %collective-permute-start.1 = (bf16[2,128,512]{2,1,0:T(8,128)(2,1)S(1)}, bf16[2,128,512]{2,1,0:T(8,128)(2,1)S(1)}, u32[]{:S(2)}, u32[]{:S(2)}) collective-permute-start(bf16[2,128,512]{2,1,0:T(8,128)(2,1)S(1)} %get-tuple-element.31), channel_id=1, source_target_pairs={{0,1},{1,0},{2,3},{3,2},{4,5},{5,4},{6,7},{7,6},{8,9},{9,8},{10,11... | collective-permute-start | bytes 786440 | tf_op jit(solution)/shard_map/ppermute | solution.py:192
  15.7 6.4 %collective-permute-start.7 = (bf16[1,128,512]{2,1,0:T(8,128)(2,1)S(1)}, bf16[1,128,512]{2,1,0:T(8,128)(2,1)S(1)}, u32[]{:S(2)}, u32[]{:S(2)}) collective-permute-start(bf16[1,128,512]{2,1,0:T(8,128)(2,1)S(1)} %get-tuple-element.43), channel_id=1, source_target_pairs={{0,2},{1,3},{2,0},{3,1},{4,6},{5,7},{6,4},{7,5},{8,10},{9,11},{10,... | collective-permute-start | bytes 393224 | tf_op jit(solution)/shard_map/ppermute | solution.py:192
  18.1 6.3 %collective-permute-start.4 = (bf16[1,128,512]{2,1,0:T(8,128)(2,1)S(1)}, bf16[1,128,512]{2,1,0:T(8,128)(2,1)S(1)}, u32[]{:S(2)}, u32[]{:S(2)}) collective-permute-start(bf16[1,128,512]{2,1,0:T(8,128)(2,1)S(1)} %get-tuple-element.38), channel_id=1, source_target_pairs={{0,2},{1,3},{2,0},{3,1},{4,6},{5,7},{6,4},{7,5},{8,10},{9,11},{10,... | collective-permute-start | bytes 393224 | tf_op jit(solution)/shard_map/ppermute | solution.py:192
where the time goes:
time: 25.3 us; the launch traced here: 25.1 us
  Pallas kernels  9.9 us (39%)
  starting transfers between devices  8.01 us (32%)
  waiting for transfers between devices  6.41 us (25%)
  local copies, waits for them, and re-layouts  0.68 us (3%)
    ppermute x6, waiting for transfers between devices, swapped(): lax.ppermute(value, axis, [(i, i ^ step) for i in range(length) if i ^ st...  5.07 us
    ppermute x6, starting transfers between devices, swapped(): lax.ppermute(value, axis, [(i, i ^ step) for i in range(length) if i ^ st...  4.13 us
    ppermute x1, starting transfers between devices, body(): second = lax.ppermute(second, 'gx', uneven + [(j, i) for i, j in uneven])  2.32 us
    pallas_call x1, Pallas kernels, body(): pl.pallas_call(functools.partial(own_kernel, parts), out_shape=(jax.Shape...  2.28 us
    pallas_call x3, Pallas kernels, written(): pl.pallas_call(functools.partial(write_kernel, order), out_shape=(whole,...  2.23 us
    pallas_call x2, Pallas kernels, body(): pl.pallas_call(functools.partial(ghost_kernel, order), out_shape=partial,...  2.1 us
    pallas_call x1, Pallas kernels, body(): pl.pallas_call(pack_kernel, out_shape=(packed, packed), in_specs=[HBM] *...  1.76 us
    ppermute x1, starting transfers between devices, body(): first = lax.ppermute(first, 'gx', even + [(j, i) for i, j in even])  1.56 us
  transfers between devices with their start and end apart: 8, of which 4 were waited for; matrix products, arithmetic and copies ran while one was open for 0% of the time, Pallas kernels for 29%

commit v1 on v0

--- a/solution.py
+++ b/solution.py
@@ -79,7 +79,7 @@
     count = sends.shape[0] // 2
     size = p_ref.shape[1]
     slots = pcol.shape[0]
-    starts = ((1 - odd) * count, odd * count)
+    starts = (odd * count, (1 - odd) * count)
     tail = packed_ref.shape[1] - count * size
     which = lax.broadcasted_iota(jnp.int32, (tail, packed_ref.shape[2]), 0)
     for i, start in enumerate(starts):
@@ -130,7 +130,7 @@
         limit = jnp.where(mush[n] > 0, KA, KS)
         at = slice(n * size, (n + 1) * size)
         for order in range(2):
-            right = odd if order else 1 - odd
+            right = 1 - odd if order else odd
             base = rows + right * (width // size)
             cols = [jnp.where(k < limit, acol[k, 0, n] - base, -1) for k in range(KA)]
             masks = masks_at(cols, size, jnp.int32)
@@ -176,7 +176,7 @@
     sum_ref, sem = refs[-2:]
     out_ref = refs[0 if order is None else 1]
     odd = lax.axis_index("gx") % 2
-    third = 1 if order is None else 2 * odd if order else 2 - 2 * odd
+    third = 1 if order is None else 2 - 2 * odd if order else 2 * odd
     width = sum_ref.shape[1]
     sum_ref[...] = keep_ref[0] + recv_ref[0].astype(F32)
     spot = pl.ds(pl.multiple_of(third * width, width), width)
@@ -264,7 +264,7 @@
     )(sends, pcol, pblk)
     even = [(i, i + 1) for i in range(0, length - 1, 2)]
     uneven = [(i, i + 1) for i in range(1, length - 1, 2)]
-    first = lax.ppermute(first, "gx", even + [(j, i) for i, j in even])
+    first = lax.ppermute(first, "gx", uneven + [(j, i) for i, j in uneven])
 
     partial = (
         jax.ShapeDtypeStruct((parts // 2, share, width), F32),
@@ -284,7 +284,7 @@
         cost_estimate=SHORT,
         name="own",
     )(acol, mush, pcol, ablk, pblk, second)
-    second = lax.ppermute(second, "gx", uneven + [(j, i) for i, j in uneven])
+    second = lax.ppermute(second, "gx", even + [(j, i) for i, j in even])
     keep, recv, folds = folded(keep, send, parts)
     split = jax.ShapeDtypeStruct((2, rows * size, count * size), BF16)
     high, low = pl.pallas_call(

time: 25.3 us -> 26.5 us (1.047)
  the two profiles are of different devices: /device:TPU:24 before, /device:TPU:0 now
where the time goes in v1:
time: 26.5 us; the launch traced here: 26.3 us
  starting transfers between devices  10.9 us (41%)
  Pallas kernels  9.88 us (37%)
  waiting for transfers between devices  4.78 us (18%)
  local copies, waits for them, and re-layouts  0.65 us (2%)
    ppermute x1, starting transfers between devices, body(): second = lax.ppermute(second, 'gx', even + [(j, i) for i, j in even])  5.79 us
    ppermute x6, waiting for transfers between devices, swapped(): lax.ppermute(value, axis, [(i, i ^ step) for i in range(length) if i ^ st...  4.78 us
    ppermute x6, starting transfers between devices, swapped(): lax.ppermute(value, axis, [(i, i ^ step) for i in range(length) if i ^ st...  4.4 us
    pallas_call x1, Pallas kernels, body(): pl.pallas_call(functools.partial(own_kernel, parts), out_shape=(jax.Shape...  2.27 us
    pallas_call x3, Pallas kernels, written(): pl.pallas_call(functools.partial(write_kernel, order), out_shape=(whole,...  2.23 us
    pallas_call x2, Pallas kernels, body(): pl.pallas_call(functools.partial(ghost_kernel, order), out_shape=partial,...  2.09 us
    pallas_call x1, Pallas kernels, body(): pl.pallas_call(pack_kernel, out_shape=(packed, packed), in_specs=[HBM] *...  1.76 us
    pallas_call x1, Pallas kernels, body(): pl.pallas_call(scatter_kernel, out_shape=(split, split), in_specs=[SMEM,...  1.37 us
  transfers between devices with their start and end apart: 8, of which 4 were waited for; matrix products, arithmetic and copies ran while one was open for 0% of the time, Pallas kernels for 28%

profile of v1, /device:TPU:0, one launch (start us, length us, event | category | flops | bytes accessed | tf_op | source)
XLA Modules:
  0.0 26.3 jit_solution(183864028525334430)
XLA Ops:
  0.0 1.8 %pack.1 = (bf16[272,256]{1,0:T(8,128)(2,1)}, bf16[272,256]{1,0:T(8,128)(2,1)}) custom-call(s32[8]{0:T(128)} %bitcast.19, s32[4,8]{1,0:T(4,128)} %bitcast.15, bf16[8,64,256]{2,1,0:T(8,128)(2,1)} %bitcast.11), custom_call_target="tpu_custom_call" | custom-call | flops 10000000000 | bytes 1000000 | tf_op jit(solution)/shard_map/pack/pallas_call | solution.py:249
  1.8 0.0 copy-start.2
  1.8 0.7 %collective-permute-start.5 = (bf16[272,256]{1,0:T(8,128)(2,1)}, bf16[272,256]{1,0:T(8,128)(2,1)S(1)}, u32[]{:S(2)}, u32[]{:S(2)}) collective-permute-start(bf16[272,256]{1,0:T(8,128)(2,1)} %get-tuple-element.39), channel_id=1, source_target_pairs={{4,8},{12,16},{20,24},{8,4},{16,12},{24,20},{5,9},{13,17},{21,25},... | collective-permute-start | bytes 417800 | tf_op jit(solution)/shard_map/ppermute | solution.py:267
  2.5 0.0 copy-start.3
  2.5 0.6 %copy-done.3 = s32[1,8,4]{1,2,0:T(4,128)S(1)} copy-done((s32[1,8,4]{1,2,0:T(4,128)S(1)}, s32[1,8,4]{1,2,0:T(4,128)}, u32[]{:S(2)}) %copy-start.3) | copy-done | bytes 152
  3.2 2.3 %own.1 = (bf16[512,512]{1,0:T(8,128)(2,1)S(1)}, f32[2,128,512]{2,1,0:T(8,128)S(1)}, bf16[2,128,512]{2,1,0:T(8,128)(2,1)S(1)}, bf16[272,256]{1,0:T(8,128)(2,1)}) custom-call(s32[7,1,8]{2,1,0:T(1,128)S(1)} %bitcast.13, s32[8]{0:T(128)S(1)} %bitcast.17, s32[4,8]{1,0:T(4,128)S(1)} %bitcast.16, ...), custom_call_target="tpu_custom_call", output_to_operand_aliasing={{3}: (5, {})} | custom-call | flops 1000000000 | bytes 1000000 | tf_op jit(solution)/shard_map/own/pallas_call | solution.py:273
  5.4 5.8 %collective-permute-start = (bf16[272,256]{1,0:T(8,128)(2,1)}, bf16[272,256]{1,0:T(8,128)(2,1)S(1)}, u32[]{:S(2)}, u32[]{:S(2)}) collective-permute-start(bf16[272,256]{1,0:T(8,128)(2,1)} %get-tuple-element.28), channel_id=1, source_target_pairs={{0,4},{8,12},{16,20},{24,28},{4,0},{12,8},{20,16},{28,24},{1,5},{9... | collective-permute-start | bytes 417800 | tf_op jit(solution)/shard_map/ppermute | solution.py:287
  11.2 1.4 %scatter.1 = (bf16[2,512,256]{2,1,0:T(8,128)(2,1)S(1)}, bf16[2,512,256]{2,1,0:T(8,128)(2,1)S(1)}) custom-call(s32[7,1,8]{2,1,0:T(1,128)S(1)} %bitcast.14, s32[8]{0:T(128)S(1)} %bitcast.18, bf16[8,64,448]{2,1,0:T(8,128)(2,1)S(1)} %bitcast.10), custom_call_target="tpu_custom_call" | custom-call | flops 10000000000 | bytes 1000000 | tf_op jit(solution)/shard_map/scatter/pallas_call | solution.py:290
  12.6 0.2 collective-permute-done.2.recv_ref
  12.8 0.1 fold.3
  12.8 1.6 %collective-permute-start.3 = (bf16[1,128,512]{2,1,0:T(8,128)(2,1)S(1)}, bf16[1,128,512]{2,1,0:T(8,128)(2,1)S(1)}, u32[]{:S(2)}, u32[]{:S(2)}) collective-permute-start(bf16[1,128,512]{2,1,0:T(8,128)(2,1)S(1)} %get-tuple-element.35), channel_id=1, source_target_pairs={{0,2},{1,3},{2,0},{3,1},{4,6},{5,7},{6,4},{7,5},{8,10},{9,11},{10,... | collective-permute-start | bytes 393224 | tf_op jit(solution)/shard_map/ppermute | solution.py:192
  14.4 1.0 %ghost.3 = (f32[2,128,512]{2,1,0:T(8,128)S(1)}, bf16[2,128,512]{2,1,0:T(8,128)(2,1)S(1)}) custom-call(bf16[2,512,256]{2,1,0:T(8,128)(2,1)S(1)} %get-tuple-element.25.high_ref, bf16[2,512,256]{2,1,0:T(8,128)(2,1)S(1)} %get-tuple-element.26.low_ref, bf16[272,256]{1,0:T(8,128)(2,1)S(1)} %collective-permute-done.5.in_ref, ...), custom_call_target="tpu_custom_call" | custom-call | flops 10000000000 | bytes 1000000 | tf_op jit(solution)/shard_map/ghost/pallas_call | solution.py:303
  15.5 0.1 collective-permute-start.6
  15.6 1.0 %ghost.2 = (f32[2,128,512]{2,1,0:T(8,128)S(1)}, bf16[2,128,512]{2,1,0:T(8,128)(2,1)S(1)}) custom-call(bf16[2,512,256]{2,1,0:T(8,128)(2,1)S(1)} %get-tuple-element.25.high_ref, bf16[2,512,256]{2,1,0:T(8,128)(2,1)S(1)} %get-tuple-element.26.low_ref, bf16[272,256]{1,0:T(8,128)(2,1)S(1)} %collective-permute-done.in_ref, ...), custom_call_target="tpu_custom_call" | custom-call | flops 10000000000 | bytes 1000000 | tf_op jit(solution)/shard_map/ghost/pallas_call | solution.py:303
  16.7 0.5 %collective-permute-start.1 = (bf16[2,128,512]{2,1,0:T(8,128)(2,1)S(1)}, bf16[2,128,512]{2,1,0:T(8,128)(2,1)S(1)}, u32[]{:S(2)}, u32[]{:S(2)}) collective-permute-start(bf16[2,128,512]{2,1,0:T(8,128)(2,1)S(1)} %get-tuple-element.31), channel_id=1, source_target_pairs={{0,1},{1,0},{2,3},{3,2},{4,5},{5,4},{6,7},{7,6},{8,9},{9,8},{10,11... | collective-permute-start | bytes 786440 | tf_op jit(solution)/shard_map/ppermute | solution.py:192
  17.2 0.6 %collective-permute-start.7 = (bf16[1,128,512]{2,1,0:T(8,128)(2,1)S(1)}, bf16[1,128,512]{2,1,0:T(8,128)(2,1)S(1)}, u32[]{:S(2)}, u32[]{:S(2)}) collective-permute-start(bf16[1,128,512]{2,1,0:T(8,128)(2,1)S(1)} %get-tuple-element.43), channel_id=1, source_target_pairs={{0,2},{1,3},{2,0},{3,1},{4,6},{5,7},{6,4},{7,5},{8,10},{9,11},{10,... | collective-permute-start | bytes 393224 | tf_op jit(solution)/shard_map/ppermute | solution.py:192
  17.8 0.9 %collective-permute-done.3.recv_ref = bf16[1,128,512]{2,1,0:T(8,128)(2,1)S(1)} collective-permute-done((bf16[1,128,512]{2,1,0:T(8,128)(2,1)S(1)}, bf16[1,128,512]{2,1,0:T(8,128)(2,1)S(1)}, u32[]{:S(2)}, u32[]{:S(2)}) %collective-permute-start.3) | collective-permute-done | bytes 131104 | tf_op jit(solution)/shard_map/ppermute | solution.py:192
  18.7 0.7 %write.3 = (f32[128,1536]{1,0:T(8,128)}, f32[8,128]{1,0:T(8,128)S(1)}) custom-call(f32[1,128,512]{2,1,0:T(8,128)S(1)} %get-tuple-element.34.keep_ref.refs_0_, bf16[1,128,512]{2,1,0:T(8,128)(2,1)S(1)} %collective-permute-done.3.recv_ref), custom_call_target="tpu_custom_call" | custom-call | flops 10000000000 | bytes 1000000 | tf_op jit(solution)/shard_map/write/pallas_call | solution.py:222
  19.4 0.1 fold.4
  19.5 1.6 %collective-permute-start.4 = (bf16[1,128,512]{2,1,0:T(8,128)(2,1)S(1)}, bf16[1,128,512]{2,1,0:T(8,128)(2,1)S(1)}, u32[]{:S(2)}, u32[]{:S(2)}) collective-permute-start(bf16[1,128,512]{2,1,0:T(8,128)(2,1)S(1)} %get-tuple-element.38), channel_id=1, source_target_pairs={{0,2},{1,3},{2,0},{3,1},{4,6},{5,7},{6,4},{7,5},{8,10},{9,11},{10,... | collective-permute-start | bytes 393224 | tf_op jit(solution)/shard_map/ppermute | solution.py:192
  21.1 2.6 %collective-permute-done.7.recv_ref = bf16[1,128,512]{2,1,0:T(8,128)(2,1)S(1)} collective-permute-done((bf16[1,128,512]{2,1,0:T(8,128)(2,1)S(1)}, bf16[1,128,512]{2,1,0:T(8,128)(2,1)S(1)}, u32[]{:S(2)}, u32[]{:S(2)}) %collective-permute-start.7) | collective-permute-done | bytes 131104 | tf_op jit(solution)/shard_map/ppermute | solution.py:192
  23.6 0.7 %write.4.refs_0_ = f32[128,1536]{1,0:T(8,128)} custom-call(f32[1,128,512]{2,1,0:T(8,128)S(1)} %get-tuple-element.42.keep_ref, bf16[1,128,512]{2,1,0:T(8,128)(2,1)S(1)} %collective-permute-done.7.recv_ref, f32[128,1536]{1,0:T(8,128)} %get-tuple-element.44.refs_0_), custom_call_target="tpu_custom_call", output_to_operand_aliasing={{}: (2, {})} | custom-call | flops 10000000000 | bytes 1000000 | tf_op jit(solution)/shard_map/write/pallas_call | solution.py:222
  24.4 1.2 %collective-permute-done.4.recv_ref = bf16[1,128,512]{2,1,0:T(8,128)(2,1)S(1)} collective-permute-done((bf16[1,128,512]{2,1,0:T(8,128)(2,1)S(1)}, bf16[1,128,512]{2,1,0:T(8,128)(2,1)S(1)}, u32[]{:S(2)}, u32[]{:S(2)}) %collective-permute-start.4) | collective-permute-done | bytes 131104 | tf_op jit(solution)/shard_map/ppermute | solution.py:192
  25.6 0.7 %write.5 = f32[128,1536]{1,0:T(8,128)} custom-call(f32[1,128,512]{2,1,0:T(8,128)S(1)} %get-tuple-element.37.keep_ref, bf16[1,128,512]{2,1,0:T(8,128)(2,1)S(1)} %collective-permute-done.4.recv_ref, f32[128,1536]{1,0:T(8,128)} %write.4.refs_0_), custom_call_target="tpu_custom_call", output_to_operand_aliasing={{}: (2, {})} | custom-call | flops 10000000000 | bytes 1000000 | tf_op jit(solution)/shard_map/write/pallas_call | solution.py:222
  (13 shorter events, 0.1 us)
Async XLA Ops:
  0.0 2.5 %copy-start = (bf16[1,8,64,448]{3,2,1,0:T(8,128)(2,1)S(1)}, bf16[1,8,64,448]{3,2,1,0:T(8,128)(2,1)}, u32[]{:S(2)}) copy-start(bf16[1,8,64,448]{3,2,1,0:T(8,128)(2,1)} %param.6) | copy-start | bytes 1376260
  0.0 2.5 %copy-start.1 = (bf16[1,8,64,256]{3,2,1,0:T(8,128)(2,1)S(1)}, bf16[1,8,64,256]{3,2,1,0:T(8,128)(2,1)}, u32[]{:S(2)}) copy-start(bf16[1,8,64,256]{3,2,1,0:T(8,128)(2,1)} %param.9) | copy-start | bytes 786436
  1.8 0.7 %copy-start.2 = (s32[1,8,7]{1,0,2:T(1,128)S(1)}, s32[1,8,7]{1,0,2:T(1,128)}, u32[]{:S(2)}) copy-start(s32[1,8,7]{1,0,2:T(1,128)} %param.7) | copy-start | bytes 676
  1.8 12.6 %collective-permute-start.5 = (bf16[272,256]{1,0:T(8,128)(2,1)}, bf16[272,256]{1,0:T(8,128)(2,1)S(1)}, u32[]{:S(2)}, u32[]{:S(2)}) collective-permute-start(bf16[272,256]{1,0:T(8,128)(2,1)} %get-tuple-element.39), channel_id=1, source_target_pairs={{4,8},{12,16},{20,24},{8,4},{16,12},{24,20},{5,9},{13,17},{21,25},... | collective-permute-start | bytes 417800 | tf_op jit(solution)/shard_map/ppermute | solution.py:267
  2.5 0.7 %copy-start.3 = (s32[1,8,4]{1,2,0:T(4,128)S(1)}, s32[1,8,4]{1,2,0:T(4,128)}, u32[]{:S(2)}) copy-start(s32[1,8,4]{1,2,0:T(4,128)} %param.10) | copy-start | bytes 388
  2.5 0.7 %copy-start.4 = (s32[1,8]{1,0:T(1,128)S(1)}, s32[1,8]{1,0:T(1,128)}, u32[]{:S(2)}) copy-start(s32[1,8]{1,0:T(1,128)} %param.8) | copy-start | bytes 100
  5.4 10.2 %collective-permute-start = (bf16[272,256]{1,0:T(8,128)(2,1)}, bf16[272,256]{1,0:T(8,128)(2,1)S(1)}, u32[]{:S(2)}, u32[]{:S(2)}) collective-permute-start(bf16[272,256]{1,0:T(8,128)(2,1)} %get-tuple-element.28), channel_id=1, source_target_pairs={{0,4},{8,12},{16,20},{24,28},{4,0},{12,8},{20,16},{28,24},{1,5},{9... | collective-permute-start | bytes 417800 | tf_op jit(solution)/shard_map/ppermute | solution.py:287
  11.2 1.5 %collective-permute-start.2 = (bf16[2,128,512]{2,1,0:T(8,128)(2,1)S(1)}, bf16[2,128,512]{2,1,0:T(8,128)(2,1)S(1)}, u32[]{:S(2)}, u32[]{:S(2)}) collective-permute-start(bf16[2,128,512]{2,1,0:T(8,128)(2,1)S(1)} %get-tuple-element.33), channel_id=1, source_target_pairs={{0,1},{1,0},{2,3},{3,2},{4,5},{5,4},{6,7},{7,6},{8,9},{9,8},{10,11... | collective-permute-start | bytes 786440 | tf_op jit(solution)/shard_map/ppermute | solution.py:192
  12.8 5.8 %collective-permute-start.3 = (bf16[1,128,512]{2,1,0:T(8,128)(2,1)S(1)}, bf16[1,128,512]{2,1,0:T(8,128)(2,1)S(1)}, u32[]{:S(2)}, u32[]{:S(2)}) collective-permute-start(bf16[1,128,512]{2,1,0:T(8,128)(2,1)S(1)} %get-tuple-element.35), channel_id=1, source_target_pairs={{0,2},{1,3},{2,0},{3,1},{4,6},{5,7},{6,4},{7,5},{8,10},{9,11},{10,... | collective-permute-start | bytes 393224 | tf_op jit(solution)/shard_map/ppermute | solution.py:192
  15.5 1.7 %collective-permute-start.6 = (bf16[2,128,512]{2,1,0:T(8,128)(2,1)S(1)}, bf16[2,128,512]{2,1,0:T(8,128)(2,1)S(1)}, u32[]{:S(2)}, u32[]{:S(2)}) collective-permute-start(bf16[2,128,512]{2,1,0:T(8,128)(2,1)S(1)} %get-tuple-element.41), channel_id=1, source_target_pairs={{0,1},{1,0},{2,3},{3,2},{4,5},{5,4},{6,7},{7,6},{8,9},{9,8},{10,11... | collective-permute-start | bytes 786440 | tf_op jit(solution)/shard_map/ppermute | solution.py:192
  16.7 2.7 %collective-permute-start.1 = (bf16[2,128,512]{2,1,0:T(8,128)(2,1)S(1)}, bf16[2,128,512]{2,1,0:T(8,128)(2,1)S(1)}, u32[]{:S(2)}, u32[]{:S(2)}) collective-permute-start(bf16[2,128,512]{2,1,0:T(8,128)(2,1)S(1)} %get-tuple-element.31), channel_id=1, source_target_pairs={{0,1},{1,0},{2,3},{3,2},{4,5},{5,4},{6,7},{7,6},{8,9},{9,8},{10,11... | collective-permute-start | bytes 786440 | tf_op jit(solution)/shard_map/ppermute | solution.py:192
  17.2 6.4 %collective-permute-start.7 = (bf16[1,128,512]{2,1,0:T(8,128)(2,1)S(1)}, bf16[1,128,512]{2,1,0:T(8,128)(2,1)S(1)}, u32[]{:S(2)}, u32[]{:S(2)}) collective-permute-start(bf16[1,128,512]{2,1,0:T(8,128)(2,1)S(1)} %get-tuple-element.43), channel_id=1, source_target_pairs={{0,2},{1,3},{2,0},{3,1},{4,6},{5,7},{6,4},{7,5},{8,10},{9,11},{10,... | collective-permute-start | bytes 393224 | tf_op jit(solution)/shard_map/ppermute | solution.py:192
  19.5 6.1 %collective-permute-start.4 = (bf16[1,128,512]{2,1,0:T(8,128)(2,1)S(1)}, bf16[1,128,512]{2,1,0:T(8,128)(2,1)S(1)}, u32[]{:S(2)}, u32[]{:S(2)}) collective-permute-start(bf16[1,128,512]{2,1,0:T(8,128)(2,1)S(1)} %get-tuple-element.38), channel_id=1, source_target_pairs={{0,2},{1,3},{2,0},{3,1},{4,6},{5,7},{6,4},{7,5},{8,10},{9,11},{10,... | collective-permute-start | bytes 393224 | tf_op jit(solution)/shard_map/ppermute | solution.py:192
